TPU v7x, 256 devices: a whole 4x4x8 slice. The times are simulated.
256 devices in a mesh: dp: 8 (over y, core), layer: 8 (over z), tensor: 4 (over x).
Axes of the slice: x: 4, y: 4, z: 8, core: 2. Of those that a mesh axis runs over, the one named last changes fastest.
Arguments:
- train_acts: bfloat16 [8, 1024, 8192], P('layer', ('dp', 'tensor')), may hold values from -6 to 6
- train_grads: bfloat16 [8, 1024, 14336], P('layer', ('dp', 'tensor')), may hold values from -6 to 6
- query_acts: bfloat16 [8, 512, 8192], P('layer', ('dp', 'tensor')), may hold values from -6 to 6
- query_grads: bfloat16 [8, 512, 14336], P('layer', ('dp', 'tensor')), may hold values from -6 to 6
- in_basis: bfloat16 [8, 8192, 8192], P('layer', None, ('dp', 'tensor')), may hold values from -0.0625 to 0.0625
- out_basis: bfloat16 [8, 14336, 128], P('layer', 'tensor'), may hold values from -0.046875 to 0.046875
- eig_values: float32 [8, 128, 8192], P('layer', None, ('dp', 'tensor')), may hold values from 0.0003 to 30
- vote_of_query: int32 [64], replicated, may hold values from 0 to 7
Outputs:
- scores: float32 [8, 8], replicated
All inputs are finite; a program needn't handle non-finite values.
Results may differ from a plain program's by a relative error of at most 0.0056.
Values may be sent and summed in bfloat16 or wider, within the bound.
No kernel may reach another device: no remote copies, remote signals or barrier semaphores. Data moves between devices by JAX's collectives and lax.ppermute only.
A program may use at most 128 MiB of HBM per device.

v0:
```python
import math

import jax
import jax.numpy as jnp
from jax import lax
from jax.sharding import PartitionSpec as P

QT = 8
SEQ_TOK = 128
VOTES = 8


def shards(
    train_acts, train_grads, query_acts, query_grads, in_basis, out_basis, eig_values, vote_of_query
):
    train_local = train_acts.shape[1]
    rows_local = train_local + query_acts.shape[1]
    features = jnp.concatenate([train_acts[0], query_acts[0]], axis=0)
    grad_rows = jnp.concatenate([train_grads[0], query_grads[0]], axis=0)
    basis_in = in_basis[0]
    basis_out = out_basis[0]
    eig_local = eig_values[0]
    width_out = basis_out.shape[1]
    width_in = basis_in.shape[0]
    column_count = basis_in.shape[1]
    queries = vote_of_query.shape[0]
    out_local = jnp.dot(
        grad_rows,
        lax.all_gather(basis_out, "tensor", axis=0, tiled=True),
        preferred_element_type=jnp.float32,
    )
    all_out = lax.all_gather(out_local.astype(jnp.bfloat16), ("dp", "tensor"), axis=0, tiled=True)
    all_in = jnp.dot(
        lax.all_gather(features, ("dp", "tensor"), axis=0, tiled=True),
        basis_in,
        preferred_element_type=jnp.float32,
    ).astype(jnp.bfloat16)
    eig_sum = lax.psum(jnp.sum(eig_local), ("dp", "tensor"))
    damping = 0.1 * eig_sum / (eig_local.shape[0] * width_in)
    device_count = all_out.shape[0] // rows_local
    out_split = all_out.reshape(device_count, rows_local, width_out)
    in_split = all_in.reshape(device_count, rows_local, column_count)
    train_out = out_split[:, :train_local].reshape(-1, width_out)
    query_out = out_split[:, train_local:].reshape(queries, QT, width_out)
    train_in = in_split[:, :train_local].reshape(-1, column_count)
    query_in = in_split[:, train_local:].reshape(queries, QT, column_count)
    query_rot = jnp.einsum("qts,qtd->qsd", query_out, query_in, preferred_element_type=jnp.float32)
    precond = (
        (query_rot / (eig_local + damping))
        .astype(jnp.bfloat16)
        .reshape(queries * width_out, column_count)
    )
    train_count = train_in.shape[0]
    block_rows = math.gcd(train_count, 512)
    score_scale = 1.0 / math.sqrt(width_out * width_in * lax.axis_size("layer") * queries)

    def block_scores(blocks):
        rows_in, rows_out = blocks
        mixed_rows = lax.dot_general(
            rows_in, precond, (((1,), (1,)), ((), ())), preferred_element_type=jnp.float32
        )
        mixed_rows = mixed_rows.reshape(block_rows, queries, width_out)
        return jnp.einsum("tqs,ts->tq", mixed_rows, rows_out.astype(jnp.float32))

    partial_scores = lax.map(
        block_scores,
        (
            train_in.reshape(-1, block_rows, column_count),
            train_out.reshape(-1, block_rows, width_out),
        ),
    )
    partial_scores = partial_scores.reshape(train_count, queries) * score_scale
    onehot = (vote_of_query[None, :] == jnp.arange(VOTES)[:, None]).astype(jnp.float32)
    token_totals = lax.psum(partial_scores, ("dp", "layer", "tensor"))
    per_seq = token_totals.reshape(-1, SEQ_TOK, queries).sum(axis=1)
    return jnp.dot(onehot, per_seq.T, precision=lax.Precision.HIGHEST)


def solution(mesh):
    placed = (
        P("layer", ("dp", "tensor"), None),
        P("layer", ("dp", "tensor"), None),
        P("layer", ("dp", "tensor"), None),
        P("layer", ("dp", "tensor"), None),
        P("layer", None, ("dp", "tensor")),
        P("layer", "tensor", None),
        P("layer", None, ("dp", "tensor")),
        P(),
    )
    return jax.shard_map(shards, mesh=mesh, in_specs=placed, out_specs=P(), check_vma=False)
```

profile of v0, /device:TPU:2, one launch (start us, length us, event | category | flops | bytes accessed | tf_op | source)
XLA Modules:
  0.0 457.8 jit_solution(10894534483957530672)
XLA Ops:
  6.5 0.7 all-gather.6.cloned.1.call-update
  7.3 0.0 all-gather.4.cloned.1.call-start
  7.3 2.1 pad_maximum_fusion
  9.4 0.0 all-gather.4.cloned.1.call-update
  9.4 0.0 all-reduce.2.cloned.1.call-start
  9.4 1.5 reduce_sum.18
  11.0 66.4 %psum.14 = f32[]{:T(128)} all-reduce(f32[]{:T(128)} %reduce_sum.18), channel_id=1, replica_groups=mesh['dp'=8,'layer'=8,'tensor'=4] {'dp','tensor'}, use_global_device_ids=true, to_apply=%region_1.0 | all-reduce | flops 1 | bytes 8 | tf_op jit(solution)/shard_map/psum | solution.py:38
  78.0 0.9 add_bitcast_fusion
  78.9 0.0 all-gather.6.cloned.1.call-done
  79.0 3.2 fusion.17
  82.2 45.1 %all_gather.11 = bf16[1536,128]{1,0:T(8,128)(2,1)S(1)} all-gather(bf16[48,128]{1,0:T(8,128)(2,1)S(1)} %fusion.17), channel_id=1, replica_groups=mesh['dp'=8,'layer'=8,'tensor'=4] {'dp','tensor'}, dimensions={0}, use_global_device_ids=true | all-gather | bytes 405504 | tf_op jit(solution)/shard_map/all_gather | solution.py:32
  127.3 32.7 %all-gather.4.cloned.1.call-done = bf16[1536,8192]{1,0:T(8,128)(2,1)} async-done(((bf16[48,8192]{1,0:T(8,128)(2,1)}), bf16[1536,8192]{1,0:T(8,128)(2,1)}) %all-gather.4.cloned.1.call-update) | async-done | bytes 25165840 | tf_op jit(solution)/shard_map/all_gather | solution.py:34
  160.1 12.8 %fusion.11 = bf16[1536,256]{1,0:T(8,128)(2,1)S(1)} fusion(bf16[1536,8192]{1,0:T(8,128)(2,1)} %all-gather.4.cloned.1.call-done, bf16[1,8192,256]{2,1,0:T(8,128)(2,1)} %param.14), kind=kOutput, calls=%fused_computation.14 | convolution fusion | flops 6442844160 | bytes 30146560 | tf_op jit(solution)/shard_map/dot_general | solution.py:33
  172.9 0.1 slice.16
  172.9 3.2 divide_convert_fusion
  176.1 20.0 %while.10 = (s32[]{:T(128)}, f32[2,512,64]{2,1,0:T(8,128)S(1)}, bf16[2,512,256]{2,1,0:T(8,128)(2,1)S(1)}, bf16[8192,256]{1,0:T(8,128)(2,1)}, bf16[2,512,128]{2,1,0:T(8,128)(2,1)S(1)}, /*index=5*/s32[]{:T(128)}) while((s32[]{:T(128)}, f32[2,512,64]{2,1,0:T(8,128)S(1)}, bf16[2,512,256]{2,1,0:T(8,128)(2,1)S(1)}, bf16[8192,256]{1,0:T(8,128)(2,1)}, ...), condition=%wide.region_3.4_spmd, body=%wide.region_2.3_spmd.sunk | while | flops 2155872256 | bytes 22282320 | solution.py:65
  176.1 4.8 %fusion.40 = bf16[512,64,128]{2,0,1:T(8,128)(2,1)S(1)} fusion(bf16[64,128,256]{2,1,0:T(8,128)(2,1)} %bitcast.53, bf16[2,512,256]{2,1,0:T(8,128)(2,1)S(1)} %get-tuple-element.88, s32[]{:T(128)} %get-tuple-element.80), kind=kOutput, calls=%fused_computation.3.clone.1 | convolution fusion | flops 2147483648 | bytes 12845060 | tf_op jit(solution)/shard_map/while/body/eval_jaxpr/dot_general | solution.py:59
  181.0 5.1 %fusion.41 = f32[512,1,64]{2,1,0:T(1,128)S(1)} fusion(bf16[512,64,128]{2,0,1:T(8,128)(2,1)S(1)} %fusion.40, bf16[512,128,1]{1,0,2:T(8,128)(2,1)S(1)} %dynamic-slice_bitcast_fusion.2), kind=kOutput, calls=%fused_computation.clone.1 | convolution fusion | flops 8388608 | bytes 8650752 | tf_op jit(solution)/shard_map/while/body/eval_jaxpr/tqs,ts->tq/dot_general | solution.py:63
  186.1 4.8 %fusion.40 = bf16[512,64,128]{2,0,1:T(8,128)(2,1)S(1)} fusion(bf16[64,128,256]{2,1,0:T(8,128)(2,1)} %bitcast.53, bf16[2,512,256]{2,1,0:T(8,128)(2,1)S(1)} %get-tuple-element.88, s32[]{:T(128)} %get-tuple-element.80), kind=kOutput, calls=%fused_computation.3.clone.1 | convolution fusion | flops 2147483648 | bytes 12845060 | tf_op jit(solution)/shard_map/while/body/eval_jaxpr/dot_general | solution.py:59
  191.0 5.1 %fusion.41 = f32[512,1,64]{2,1,0:T(1,128)S(1)} fusion(bf16[512,64,128]{2,0,1:T(8,128)(2,1)S(1)} %fusion.40, bf16[512,128,1]{1,0,2:T(8,128)(2,1)S(1)} %dynamic-slice_bitcast_fusion.2), kind=kOutput, calls=%fused_computation.clone.1 | convolution fusion | flops 8388608 | bytes 8650752 | tf_op jit(solution)/shard_map/while/body/eval_jaxpr/tqs,ts->tq/dot_general | solution.py:63
  196.1 0.9 broadcast_multiply_fusion
  197.0 252.4 %all-reduce.2.cloned.1.call-done = f32[8,128,64]{2,1,0:T(8,128)} async-done(((f32[8,128,64]{2,1,0:T(8,128)}), f32[8,128,64]{2,1,0:T(8,128)}) %all-reduce.2.cloned.1.call-update) | async-done | bytes 262160 | tf_op jit(solution)/shard_map/psum | solution.py:74
  449.4 1.1 reduce_sum.19
  450.5 0.7 fusion.22
  (12 shorter events, 0.2 us)
Async XLA Ops:
  6.5 72.4 %all-gather.6.cloned.1.call-start = ((), (), s32[]{:S(2)}) async-start(), calls=%async_computation.2 | async-start | bytes 4587520 | tf_op jit(solution)/shard_map/all_gather | solution.py:29
  7.3 152.8 %all-gather.4.cloned.1.call-start = ((), (), s32[]{:S(2)}) async-start(), calls=%async_computation | async-start | bytes 25952256 | tf_op jit(solution)/shard_map/all_gather | solution.py:34
  9.4 440.0 %all-reduce.2.cloned.1.call-start = ((), (), s32[]{:S(2)}) async-start(), calls=%async_computation.1 | async-start | bytes 1048576 | tf_op jit(solution)/shard_map/psum | solution.py:74
  176.1 274.3 %copy-start = (s32[64]{0:T(128)S(1)}, s32[64]{0:T(128)}, u32[]{:S(2)}) copy-start(s32[64]{0:T(128)} %param.17) | copy-start | bytes 772
Sparse Core Ops, SparseCore 0:
  9.2 49.3 all-gather.5
  61.1 98.8 all-gather.3
  197.1 252.2 all-reduce.1
where the time goes:
time: 458 us
  waiting for transfers between devices  286 us (62%)
  blocking collectives  111 us (24%)
  matrix products  39.8 us (9%)
  between operations  13.8 us (3%)
  other arithmetic  6.47 us (1%)
    psum x1, waiting for transfers between devices, shards(): token_totals = lax.psum(partial_scores, ('dp', 'layer', 'tensor'))  252 us
    psum x1, blocking collectives, shards(): eig_sum = lax.psum(jnp.sum(eig_local), ('dp', 'tensor'))  66.4 us
    all_gather x1, blocking collectives, shards(): lax.all_gather(out_local.astype(jnp.bfloat16), ('dp', 'tensor'), axis=0,...  45.1 us
    all_gather x1, waiting for transfers between devices, shards(): lax.all_gather(features, ('dp', 'tensor'), axis=0, tiled=True)  32.7 us
    dot_general x1, matrix products, shards(): jnp.dot(lax.all_gather(features, ('dp', 'tensor'), axis=0, tiled=True), b...  12.8 us
    dot_general x2, matrix products, block_scores(): return jnp.einsum('tqs,ts->tq', mixed_rows, rows_out.astype(jnp.float32))  10.2 us
    dot_general x2, matrix products, block_scores(): lax.dot_general(rows_in, precond, (((1,), (1,)), ((), ())), preferred_ele...  9.62 us
  transfers between devices with their start and end apart: 3, of which 2 were waited for; matrix products, arithmetic and copies ran while one was open for 2% of the time, Pallas kernels for 0%

commit v1 on v0

v1 whole, which is shorter than its diff:
```python
import math

import jax
import jax.numpy as jnp
import numpy as np
from jax import lax
from jax.experimental import pallas as pl
from jax.experimental.pallas import tpu as pltpu
from jax.sharding import Mesh
from jax.sharding import PartitionSpec as P

QT = 8
SEQ_TOK = 128
VOTES = 8
RING = 4


def shift(a, axis, step):
    n = lax.axis_size(axis)
    return lax.ppermute(a, axis, [(i, (i + step) % n) for i in range(n)])


class Rows:
    def __init__(self, parts):
        self.parts = parts

    def cut(self, low, high):
        parts, at = [], 0
        for dx, dy, first, count in self.parts:
            a, b = max(low, at), min(high, at + count)
            if a < b:
                parts.append((dx, dy, first + a - at, b - a))
            at += count
        return Rows(parts)


def cut(a, low, high):
    return a.cut(low, high) if isinstance(a, Rows) else lax.slice_in_dim(a, low, high, axis=0)


def cat(parts):
    if isinstance(parts[0], Rows):
        return Rows([entry for part in parts for entry in part.parts])
    return jnp.concatenate(parts, axis=0)


def send(a, axis, step):
    if isinstance(a, Rows):
        mx, my = (step, 0) if axis == "tensor" else (0, step)
        return Rows([((dx - mx) % RING, (dy - my) % RING, f, n) for dx, dy, f, n in a.parts])
    return shift(a, axis, step)


def spread_1(o):
    return [send(o, "tensor", 1), send(o, "tensor", -1), send(o, "y", 1), send(o, "y", -1)]


def spread_2(r1, rows, half):
    west, east, south, north = r1
    q1, q2 = half // 2, (rows - half) // 2
    first = lambda a: [cut(a, 0, q1), cut(a, half, half + q2)]
    second = lambda a: [cut(a, q1, half), cut(a, half + q2, rows)]
    tops = lambda a: cut(a, 0, half)
    tails = lambda a: cut(a, half, rows)
    return [
        send(cat(first(west) + [tails(north), tails(south)]), "tensor", 1),
        send(cat(second(east) + [tails(north), tails(south)]), "tensor", -1),
        send(cat(first(south) + [tops(east), tops(west)]), "y", 1),
        send(cat(second(north) + [tops(east), tops(west)]), "y", -1),
    ]


def spread_3(r2, rows, half):
    a, b, c, d = r2
    q1, q2 = half // 2, (rows - half) // 2
    m = q1 + q2
    far_y = [cut(c, q1, m), cut(d, q1, m)]
    far_x = [cut(a, 0, q1), cut(b, 0, q1)]
    return [
        send(cat(far_y + [cut(a, m, m + q2), cut(a, m + 2 * q2, m + 3 * q2)]), "tensor", 1),
        send(cat(far_y + [cut(b, m + q2, m + 2 * q2), cut(b, m + 3 * q2, m + 4 * q2)]), "tensor", -1),
        send(cat(far_x + [cut(c, m, m + q1), cut(c, m + 2 * q1, m + 3 * q1)]), "y", 1),
        send(cat(far_x + [cut(d, m + q1, m + 2 * q1), cut(d, m + 3 * q1, m + 4 * q1)]), "y", -1),
    ]


def spread_4(r3, rows, half):
    e, f, g, h = r3
    q1, q2 = half // 2, (rows - half) // 2
    return [
        send(cut(e, 0, q2), "tensor", 1),
        send(cut(f, q2, 2 * q2), "tensor", -1),
        send(cut(g, 0, q1), "y", 1),
        send(cut(h, q1, 2 * q1), "y", -1),
    ]


def order_of(rows, half):
    own = Rows([(0, 0, 0, rows)])
    r1 = spread_1(own)
    r2 = spread_2(r1, rows, half)
    r3 = spread_3(r2, rows, half)
    r4 = spread_4(r3, rows, half)
    rounds = []
    for messages in ([own] + r1, r2, r3, r4):
        rounds.append(
            np.array([(dx, dy, f + i) for m in messages for dx, dy, f, n in m.parts for i in range(n)], np.int32)
        )
    return rounds


def score_kernel(acts, basis, precond, weight, scores, sums):
    step, seqs = pl.program_id(0), acts.shape[0] // SEQ_TOK
    rows_in = jnp.dot(acts[...], basis[...], preferred_element_type=jnp.float32).astype(jnp.bfloat16)
    mixed = lax.dot_general(
        rows_in, precond[...], (((1,), (1,)), ((), ())), preferred_element_type=jnp.float32
    )
    mixed = mixed * jnp.concatenate([weight[...].astype(jnp.float32)] * VOTES, axis=1)
    for i in range(seqs):
        part = mixed[i * SEQ_TOK : (i + 1) * SEQ_TOK]
        sums[pl.ds(step * seqs + i, 1), :] = jnp.sum(part, axis=0, keepdims=True)

    @pl.when(step == pl.num_programs(0) - 1)
    def _():
        width = weight.shape[1]
        total = sums[...]
        scores[...] = jnp.concatenate(
            [jnp.sum(total[:, v * width : (v + 1) * width], axis=1, keepdims=True) for v in range(VOTES)],
            axis=1,
        )


def score_rows(acts, basis, precond, weight):
    tokens, width_in = acts.shape
    rows = 2 * SEQ_TOK
    whole = lambda a: pl.BlockSpec(a.shape, lambda i: (0, 0), pipeline_mode=pl.Buffered(1))
    return pl.pallas_call(
        score_kernel,
        grid=(tokens // rows,),
        in_specs=[
            pl.BlockSpec((rows, width_in), lambda i: (i, 0)),
            whole(basis),
            whole(precond),
            pl.BlockSpec((rows, weight.shape[1]), lambda i: (i, 0)),
        ],
        out_specs=pl.BlockSpec((tokens // SEQ_TOK, VOTES), lambda i: (0, 0)),
        out_shape=jax.ShapeDtypeStruct((tokens // SEQ_TOK, VOTES), jnp.float32),
        scratch_shapes=[pltpu.VMEM((tokens // SEQ_TOK, precond.shape[0]), jnp.float32)],
        compiler_params=pltpu.CompilerParams(vmem_limit_bytes=40 * 1024 * 1024),
        cost_estimate=pl.CostEstimate(
            flops=2 * tokens * basis.shape[1] * (width_in + precond.shape[0]),
            bytes_accessed=2 * (acts.size + basis.size + precond.size),
            transcendentals=0,
        ),
    )(acts, basis, precond, weight)


def shards(
    train_acts, train_grads, query_acts, query_grads, in_basis, out_basis, eig_values, vote_of_query
):
    core, x, y = lax.axis_index("core"), lax.axis_index("tensor"), lax.axis_index("y")
    train_local, query_local = train_acts.shape[1], query_acts.shape[1]
    local = train_local + query_local
    width_in, columns = in_basis.shape[1], in_basis.shape[2]
    depth = width_in // 2
    block, width_out = out_basis.shape[1], out_basis.shape[2]
    queries = vote_of_query.shape[0]
    eig_local = eig_values[0]

    def by_core(mine, other):
        return jnp.where(core == 0, mine, other), jnp.where(core == 0, other, mine)

    def halves(a, axis):
        mine = lax.dynamic_slice_in_dim(a, core * depth, depth, axis)
        other = lax.dynamic_slice_in_dim(a, (1 - core) * depth, depth, axis)
        return by_core(mine, shift(other, "core", 1))

    train_all = lax.all_gather(train_acts[0], ("y", "core", "tensor"), axis=0, tiled=True)
    query_block = jnp.concatenate(halves(query_acts[0], 1), axis=0)
    basis_mine = lax.dynamic_slice_in_dim(in_basis[0], core * depth, depth, 0)
    basis_other = lax.dynamic_slice_in_dim(in_basis[0], (1 - core) * depth, depth, 0)
    basis = jnp.concatenate([basis_mine, shift(basis_other, "core", 1)], axis=1)

    def grads_for(dx):
        at = lax.rem(x + dx, RING) * block
        return jnp.concatenate(
            [lax.dynamic_slice_in_dim(g[0], at, block, 1) for g in (train_grads, query_grads)], axis=0
        )

    grads = [grads_for(0)] + [shift(grads_for(dx), "tensor", dx) for dx in (1, 2, 3)]
    partial = [
        jnp.dot(grads[-e % RING], out_basis[0], preferred_element_type=jnp.float32) for e in range(RING)
    ]
    eig_row = jnp.full((8, width_out), jnp.sum(eig_local), jnp.float32)
    partial = jnp.concatenate(partial + [eig_row], axis=0)
    total = partial
    for k in (1, 2, 3):
        other = shift(partial, "tensor", k)
        total = total + jnp.concatenate(
            [other[((e + k) % RING) * local : ((e + k) % RING + 1) * local] for e in range(RING)]
            + [other[RING * local :]],
            axis=0,
        )
    eig_high = total[RING * local :].astype(jnp.bfloat16)
    eig_low = (total[RING * local :] - eig_high.astype(jnp.float32)).astype(jnp.bfloat16)
    out_x = jnp.concatenate([total[: RING * local].astype(jnp.bfloat16), eig_high, eig_low], axis=0)
    pair = jnp.stack(by_core(out_x, shift(out_x, "core", 1)))
    stack = jnp.stack([pair] + [shift(pair, "y", -dy) for dy in (1, 2, 3)])
    eig_sum = jnp.sum(stack[:, :, RING * local :, 0].astype(jnp.float32)) / 8.0
    damping = 0.1 * eig_sum / (eig_local.shape[0] * width_in)
    out_rows = stack[:, :, : RING * local].reshape(RING, 2, RING, local, width_out).swapaxes(1, 2)
    out_train = out_rows[:, :, :, :train_local].reshape(-1, width_out)
    out_query = out_rows[:, :, :, train_local:].reshape(-1, width_out)

    def in_order(a, rounds, rows):
        at = np.concatenate([(r[:, 1] * RING + r[:, 0]) * rows + r[:, 2] for r in rounds])
        pick = jnp.asarray(np.eye(a.shape[0], dtype=np.float32)[at], jnp.bfloat16)
        return jnp.dot(pick, a, preferred_element_type=jnp.float32).astype(jnp.bfloat16)

    def token_ids(rounds, rows):
        all_rows = np.concatenate(rounds)
        per = rows // 2
        sx = lax.rem(x + all_rows[:, 0], RING)
        sy = lax.rem(y + all_rows[:, 1], RING)
        sc = all_rows[:, 2] // per
        return ((sy * 2 + sc) * RING + sx) * per + all_rows[:, 2] % per

    def multiply(messages):
        return jnp.dot(jnp.concatenate(messages, axis=0), basis, preferred_element_type=jnp.float32)

    q_rows, q_half = 2 * query_local, query_local
    q1 = spread_1(query_block)
    q2 = spread_2(q1, q_rows, q_half)
    q3 = spread_3(q2, q_rows, q_half)
    q4 = spread_4(q3, q_rows, q_half)

    q_order = order_of(q_rows, q_half)
    q_in = jnp.concatenate([multiply([query_block] + q1), multiply(q2), multiply(q3 + q4)], axis=0)
    query_in = (q_in[:, :columns] + shift(q_in[:, columns:], "core", 1)).astype(jnp.bfloat16)
    query_id = token_ids(q_order, q_rows) // QT
    votes = jnp.sum(
        jnp.where(query_id[:, None] == jnp.arange(queries)[None, :], vote_of_query[None, :], 0), axis=1
    )
    by_vote = (votes[:, None] == jnp.arange(VOTES)[None, :]).astype(jnp.bfloat16)
    query_out = in_order(out_query, q_order, q_rows)
    spread_out = (by_vote[:, :, None] * query_out[:, None, :]).reshape(-1, VOTES * width_out)
    query_rot = lax.dot_general(
        spread_out, query_in, (((0,), (0,)), ((), ())), preferred_element_type=jnp.float32
    )
    precond = query_rot.reshape(VOTES, width_out, columns) / (eig_local + damping)
    precond = precond.astype(jnp.bfloat16).reshape(VOTES * width_out, columns)

    every = np.array([(dx, dy, r) for dy in range(RING) for dx in range(RING) for r in range(2 * train_local)])
    tokens = every.shape[0]
    train_id = token_ids([every.astype(np.int32)], 2 * train_local)
    pick = (jnp.arange(tokens)[:, None] == train_id[None, :]).astype(jnp.bfloat16)
    train_out = jnp.dot(pick, out_train, preferred_element_type=jnp.float32).astype(jnp.bfloat16)
    score_scale = 1.0 / math.sqrt(width_out * width_in * lax.axis_size("layer") * queries)
    scores = score_rows(train_all, in_basis[0], precond, train_out).T * score_scale

    plane = ("y", "core", "tensor")
    copies = jnp.broadcast_to(scores[None], (lax.axis_size(plane),) + scores.shape)
    scores = jnp.sum(lax.all_to_all(copies, plane, 0, 0, tiled=True), axis=0)
    layers, step = lax.axis_size("layer"), 1
    while step < layers:
        scores = scores + lax.ppermute(scores, "layer", [(i, i ^ step) for i in range(layers)])
        step *= 2
    return scores


def solution(mesh):
    fine = Mesh(mesh.devices.reshape(RING, 2, -1, RING), ("y", "core", "layer", "tensor"))
    rows = ("y", "core", "tensor")
    placed = (
        P("layer", rows, None),
        P("layer", rows, None),
        P("layer", rows, None),
        P("layer", rows, None),
        P("layer", None, rows),
        P("layer", "tensor", None),
        P("layer", None, rows),
        P(),
    )
    return jax.shard_map(shards, mesh=fine, in_specs=placed, out_specs=P(), check_vma=False)
```

time: 458 us -> 163 us (0.36)
  waiting for transfers between devices: 286 us -> 24.7 us
  blocking collectives: 111 us -> 13.6 us
  starting transfers between devices: 0.08 us -> 60.1 us
  matrix products: 39.8 us -> 13.2 us
  local copies, waits for them, and re-layouts: 0.18 us -> 18.7 us
  Pallas kernels: 0 us -> 9.75 us
    psum x1 -> x0, waiting for transfers between devices: 252 us -> none  [shards(): token_totals = lax.psum(partial_scores, ('dp', 'layer', 'tensor'))]
    psum x1 -> x0, blocking collectives: 66.4 us -> none  [shards(): eig_sum = lax.psum(jnp.sum(eig_local), ('dp', 'tensor'))]
    ppermute x0 -> x32, starting transfers between devices: none -> 60.1 us  [the longest x29 46 us: shift(): return lax.ppermute(a, axis, [(i, (i + step) % n) for i in range(n)])]
    all_gather x1 -> x0, blocking collectives: 45.1 us -> none  [shards(): lax.all_gather(out_local.astype(jnp.bfloat16), ('dp', 'tensor'), axis=0,...]
    all_gather x2 -> x1, waiting for transfers between devices: 32.8 us -> 0.02 us  [shards(): lax.all_gather(train_acts[0], ('y', 'core', 'tensor'), axis=0, tiled=True)]
    dot_general x8 -> x10, matrix products: 39.8 us -> 13.2 us  [the longest x3 7.54 us: multiply(): jnp.dot(jnp.concatenate(messages, axis=0), basis, preferred_element_type=...]
    ppermute x0 -> x32, waiting for transfers between devices: none -> 23.9 us  [the longest x29 19.2 us: shift(): return lax.ppermute(a, axis, [(i, (i + step) % n) for i in range(n)])]
    all_to_all x0 -> x1, blocking collectives: none -> 13.6 us  [shards(): scores = jnp.sum(lax.all_to_all(copies, plane, 0, 0, tiled=True), axis=0)]
  transfers between devices with their start and end apart: 3 -> 33, of which waited for: 2 -> 13; matrix products, arithmetic and copies ran while one was open for 2% -> 21% of each run, Pallas kernels for 0% -> 0%
where the time goes in v1:
time: 163 us; the launch traced here: 161 us
  starting transfers between devices  60.1 us (37%)
  waiting for transfers between devices  24.7 us (15%)
  local copies, waits for them, and re-layouts  18.7 us (11%)
  between operations  15 us (9%)
  blocking collectives  13.6 us (8%)
  matrix products  13.2 us (8%)
  Pallas kernels  9.75 us (6%)
  other arithmetic  6.51 us (4%)
    ppermute x29, starting transfers between devices, shift(): return lax.ppermute(a, axis, [(i, (i + step) % n) for i in range(n)])  46 us
    ppermute x29, waiting for transfers between devices, shift(): return lax.ppermute(a, axis, [(i, (i + step) % n) for i in range(n)])  19.2 us
    ppermute x3, starting transfers between devices, shards(): lax.ppermute(scores, 'layer', [(i, i ^ step) for i in range(layers)])  14.1 us
    all_to_all x1, blocking collectives, shards(): scores = jnp.sum(lax.all_to_all(copies, plane, 0, 0, tiled=True), axis=0)  13.6 us
    pallas_call x1, Pallas kernels, score_rows(): pl.pallas_call(score_kernel, grid=(tokens // rows,), in_specs=[pl.BlockSp...  9.75 us
    unnamed x64, local copies, waits for them, and re-layouts  8.32 us
    dot_general x3, matrix products, multiply(): jnp.dot(jnp.concatenate(messages, axis=0), basis, preferred_element_type=...  7.54 us
    ppermute x3, waiting for transfers between devices, shards(): lax.ppermute(scores, 'layer', [(i, i ^ step) for i in range(layers)])  4.76 us
  transfers between devices with their start and end apart: 33, of which 13 were waited for; matrix products, arithmetic and copies ran while one was open for 21% of the time, Pallas kernels for 0%

profile of v1, /device:TPU:2, one launch (start us, length us, event | category | flops | bytes accessed | tf_op | source)
XLA Modules:
  0.0 161.5 jit_solution(15554494909199453268)
XLA Ops:
  10.4 2.3 %collective-permute-start = (bf16[48,3584]{1,0:T(8,128)(2,1)}, bf16[48,3584]{1,0:T(8,128)(2,1)}, u32[]{:S(2)}, u32[]{:S(2)}) collective-permute-start(bf16[48,3584]{1,0:T(8,128)(2,1)} %pad_maximum_fusion.14), channel_id=1, source_target_pairs={{0,3},{1,0},{2,1},{3,2},{4,7},{5,4},{6,5},{7,6},{8,11},{9,8},{10,9... | collective-permute-start | bytes 1032200 | tf_op jit(solution)/shard_map/ppermute | solution.py:20
  17.8 3.9 %dynamic-slice_bitcast_fusion.1 = (bf16[4096,256]{1,0:T(8,128)(2,1)S(1)}, bf16[4096,256]{1,0:T(8,128)(2,1)}) fusion(bf16[1,8192,256]{2,1,0:T(8,128)(2,1)} %param.21, s32[]{:T(128)S(6)} %select_n.67, s32[]{:T(128)S(6)} %select_n.68), kind=kLoop, calls=%fused_computation.5 | loop fusion | bytes 8388616 | tf_op jit(solution)/shard_map/dynamic_slice | solution.py:180
  26.8 4.2 %collective-permute-done.1 = bf16[48,3584]{1,0:T(8,128)(2,1)} collective-permute-done((bf16[48,3584]{1,0:T(8,128)(2,1)}, bf16[48,3584]{1,0:T(8,128)(2,1)}, u32[]{:S(2)}, u32[]{:S(2)}) %collective-permute-start.1) | collective-permute-done | bytes 344096 | tf_op jit(solution)/shard_map/ppermute | solution.py:20
  31.0 3.0 %collective-permute-start.14 = (bf16[32,4096]{1,0:T(8,128)(2,1)S(1)}, bf16[32,4096]{1,0:T(8,128)(2,1)S(1)}, u32[]{:S(2)}, u32[]{:S(2)}) collective-permute-start(bf16[32,4096]{1,0:T(8,128)(2,1)S(1)} %pad_maximum_fusion.17), channel_id=1, source_target_pairs={{0,192},{64,0},{128,64},{192,128},{1,193},{65,1},{129,65},{193,129... | collective-permute-start | bytes 786440 | tf_op jit(solution)/shard_map/ppermute | solution.py:20
  38.2 3.2 %collective-permute-start.4 = (f32[200,128]{1,0:T(8,128)S(1)}, f32[200,128]{1,0:T(8,128)S(1)}, u32[]{:S(2)}, u32[]{:S(2)}) collective-permute-start(f32[200,128]{1,0:T(8,128)S(1)} %constant_dynamic-update-slice_fusion), channel_id=1, source_target_pairs={{0,2},{1,3},{2,0},{3,1},{4,6},{5,7},{6,4},{7,5},{8,10},{9,11},{10,... | collective-permute-start | bytes 307208 | tf_op jit(solution)/shard_map/ppermute | solution.py:20
  42.1 2.5 %collective-permute-start.5 = (f32[200,128]{1,0:T(8,128)S(1)}, f32[200,128]{1,0:T(8,128)S(1)}, u32[]{:S(2)}, u32[]{:S(2)}) collective-permute-start(f32[200,128]{1,0:T(8,128)S(1)} %constant_dynamic-update-slice_fusion), channel_id=1, source_target_pairs={{0,3},{1,0},{2,1},{3,2},{4,7},{5,4},{6,5},{7,6},{8,11},{9,8},{10,9... | collective-permute-start | bytes 307208 | tf_op jit(solution)/shard_map/ppermute | solution.py:20
  49.4 1.9 %collective-permute-start.16 = (bf16[48,4096]{1,0:T(8,128)(2,1)S(1)}, bf16[48,4096]{1,0:T(8,128)(2,1)S(1)}, u32[]{:S(2)}, u32[]{:S(2)}) collective-permute-start(bf16[48,4096]{1,0:T(8,128)(2,1)S(1)} %get-tuple-element.34), channel_id=1, source_target_pairs={{0,1},{1,2},{2,3},{3,0},{4,5},{5,6},{6,7},{7,4},{8,9},{9,10},{10,1... | collective-permute-start | bytes 1179656 | tf_op jit(solution)/shard_map/ppermute | solution.py:20
  54.1 2.7 %collective-permute-start.7 = (bf16[2,208,128]{2,1,0:T(8,128)(2,1)S(1)}, bf16[2,208,128]{2,1,0:T(8,128)(2,1)S(1)}, u32[]{:S(2)}, u32[]{:S(2)}) collective-permute-start(bf16[2,208,128]{2,1,0:T(8,128)(2,1)S(1)} %get-tuple-element.50), channel_id=1, source_target_pairs={{0,192},{64,0},{128,64},{192,128},{1,193},{65,1},{129,65},{193,129... | collective-permute-start | bytes 319496 | tf_op jit(solution)/shard_map/ppermute | solution.py:20
  56.9 3.0 %collective-permute-start.8 = (bf16[2,208,128]{2,1,0:T(8,128)(2,1)S(1)}, bf16[2,208,128]{2,1,0:T(8,128)(2,1)S(1)}, u32[]{:S(2)}, u32[]{:S(2)}) collective-permute-start(bf16[2,208,128]{2,1,0:T(8,128)(2,1)S(1)} %get-tuple-element.50), channel_id=1, source_target_pairs={{0,128},{64,192},{128,0},{192,64},{1,129},{65,193},{129,1},{193,65... | collective-permute-start | bytes 319496 | tf_op jit(solution)/shard_map/ppermute | solution.py:20
  61.0 3.2 %collective-permute-done.16 = bf16[48,4096]{1,0:T(8,128)(2,1)S(1)} collective-permute-done((bf16[48,4096]{1,0:T(8,128)(2,1)S(1)}, bf16[48,4096]{1,0:T(8,128)(2,1)S(1)}, u32[]{:S(2)}, u32[]{:S(2)}) %collective-permute-start.16) | collective-permute-done | bytes 393248 | tf_op jit(solution)/shard_map/ppermute | solution.py:20
  67.6 2.8 %collective-permute-start.20 = (bf16[32,4096]{1,0:T(8,128)(2,1)}, bf16[32,4096]{1,0:T(8,128)(2,1)}, u32[]{:S(2)}, u32[]{:S(2)}) collective-permute-start(bf16[32,4096]{1,0:T(8,128)(2,1)} %get-tuple-element.48), channel_id=1, source_target_pairs={{0,1},{1,2},{2,3},{3,0},{4,5},{5,6},{6,7},{7,4},{8,9},{9,10},{10,1... | collective-permute-start | bytes 786440 | tf_op jit(solution)/shard_map/ppermute | solution.py:20
  70.4 2.7 %collective-permute-start.21 = (bf16[32,4096]{1,0:T(8,128)(2,1)}, bf16[32,4096]{1,0:T(8,128)(2,1)}, u32[]{:S(2)}, u32[]{:S(2)}) collective-permute-start(bf16[32,4096]{1,0:T(8,128)(2,1)} %get-tuple-element.47), channel_id=1, source_target_pairs={{0,3},{1,0},{2,1},{3,2},{4,7},{5,4},{6,5},{7,6},{8,11},{9,8},{10,9... | collective-permute-start | bytes 786440 | tf_op jit(solution)/shard_map/ppermute | solution.py:20
  73.1 1.9 %collective-permute-start.23 = (bf16[32,4096]{1,0:T(8,128)(2,1)}, bf16[32,4096]{1,0:T(8,128)(2,1)}, u32[]{:S(2)}, u32[]{:S(2)}) collective-permute-start(bf16[32,4096]{1,0:T(8,128)(2,1)} %get-tuple-element.45), channel_id=1, source_target_pairs={{0,192},{64,0},{128,64},{192,128},{1,193},{65,1},{129,65},{193,129... | collective-permute-start | bytes 786440 | tf_op jit(solution)/shard_map/ppermute | solution.py:20
  77.5 7.0 %collective-permute-done.20 = bf16[32,4096]{1,0:T(8,128)(2,1)} collective-permute-done((bf16[32,4096]{1,0:T(8,128)(2,1)}, bf16[32,4096]{1,0:T(8,128)(2,1)}, u32[]{:S(2)}, u32[]{:S(2)}) %collective-permute-start.20) | collective-permute-done | bytes 262176 | tf_op jit(solution)/shard_map/ppermute | solution.py:20
  85.3 2.0 %collective-permute-start.24 = (bf16[8,4096]{1,0:T(8,128)(2,1)S(1)}, bf16[8,4096]{1,0:T(8,128)(2,1)S(1)}, u32[]{:S(2)}, u32[]{:S(2)}) collective-permute-start(bf16[8,4096]{1,0:T(8,128)(2,1)S(1)} %slice.233), channel_id=1, source_target_pairs={{0,1},{1,2},{2,3},{3,0},{4,5},{5,6},{6,7},{7,4},{8,9},{9,10},{10,1... | collective-permute-start | bytes 196616 | tf_op jit(solution)/shard_map/ppermute | solution.py:20
  99.0 2.7 %fusion.2 = f32[192,512]{1,0:T(8,128)S(1)} fusion(bf16[48,4096]{1,0:T(8,128)(2,1)S(1)} %copy-done.11, bf16[48,4096]{1,0:T(8,128)(2,1)S(1)} %copy-done.9, bf16[48,4096]{1,0:T(8,128)(2,1)S(1)} %copy-done.15, bf16[48,4096]{1,0:T(8,128)(2,1)S(1)} %copy-done.13, bf16[4096,256]{1,0:T(8,128)(2,1)} %collective-permute-done.15, ...), kind=kOutput, calls=%fused_computation.6 | convolution fusion | flops 819986432 | bytes 6160384 | tf_op jit(solution)/shard_map/dot_general | solution.py:229
  101.7 2.4 %fusion.12 = f32[160,512]{1,0:T(8,128)S(1)} fusion(bf16[160,4096]{1,0:T(8,128)(2,1)S(1)} %copy-done.17, bf16[4096,256]{1,0:T(8,128)(2,1)} %collective-permute-done.15, bf16[4096,256]{1,0:T(8,128)(2,1)S(1)} %get-tuple-element.11), kind=kOutput, calls=%fused_computation.17 | convolution fusion | flops 679477248 | bytes 5832704 | tf_op jit(solution)/shard_map/dot_general | solution.py:229
  104.1 2.4 %fusion.11 = f32[160,512]{1,0:T(8,128)S(1)} fusion(bf16[160,4096]{1,0:T(8,128)(2,1)S(1)} %constant_dynamic-update-slice_fusion.7, bf16[4096,256]{1,0:T(8,128)(2,1)} %collective-permute-done.15, bf16[4096,256]{1,0:T(8,128)(2,1)S(1)} %get-tuple-element.11), kind=kOutput, calls=%fused_computation.16 | convolution fusion | flops 679477248 | bytes 5832704 | tf_op jit(solution)/shard_map/dot_general | solution.py:229
  109.5 2.2 %copy-done.1 = bf16[1,8192,256]{2,1,0:T(8,128)(2,1)S(1)} copy-done((bf16[1,8192,256]{2,1,0:T(8,128)(2,1)S(1)}, bf16[1,8192,256]{2,1,0:T(8,128)(2,1)}, u32[]{:S(2)}) %copy-start.1) | copy-done | bytes 4194328
  111.7 9.8 %shard_map.163 = f32[8,8]{1,0:T(8,128)S(1)} custom-call(bf16[1024,8192]{1,0:T(8,128)(2,1)} %bitcast.80, bf16[8192,256]{1,0:T(8,128)(2,1)S(1)} %bitcast.78, bf16[1024,256]{1,0:T(8,128)(2,1)S(1)} %bitcast.79, bf16[1024,128]{1,0:T(8,128)(2,1)S(1)} %fusion.13.weight), custom_call_target="tpu_custom_call" | custom-call | flops 4831838208 | bytes 21495808 | tf_op jit(solution)/shard_map/pallas_call | solution.py:137
  121.6 13.6 %all_to_all.5 = f32[32,8,8]{2,1,0:T(8,128)S(1)} all-to-all(f32[32,8,8]{2,1,0:T(8,128)S(1)} %broadcast_in_dim.19), channel_id=1, replica_groups=mesh['y'=4,'core'=2,'layer'=8,'tensor'=4] {'y','core','tensor'}, dimensions={0} | all-to-all | bytes 16384 | tf_op jit(solution)/shard_map/all_to_all | solution.py:263
  135.2 2.5 %collective-permute-start.29 = (f32[8,8]{1,0:T(8,128)S(1)}, f32[8,8]{1,0:T(8,128)S(1)}, u32[]{:S(2)}, u32[]{:S(2)}) collective-permute-start(f32[8,8]{1,0:T(8,128)S(1)} %reduce_sum.39), channel_id=1, source_target_pairs={{0,4},{4,0},{8,12},{12,8},{16,20},{20,16},{24,28},{28,24},{1,5},{5... | collective-permute-start | bytes 776 | tf_op jit(solution)/shard_map/ppermute | solution.py:266
  139.2 4.5 %collective-permute-start.30 = (f32[8,8]{1,0:T(8,128)S(1)}, f32[8,8]{1,0:T(8,128)S(1)}, u32[]{:S(2)}, u32[]{:S(2)}) collective-permute-start(f32[8,8]{1,0:T(8,128)S(1)} %add.133), channel_id=1, source_target_pairs={{0,8},{4,12},{8,0},{12,4},{16,24},{20,28},{24,16},{28,20},{1,9},{5... | collective-permute-start | bytes 776 | tf_op jit(solution)/shard_map/ppermute | solution.py:266
  145.3 7.2 %collective-permute-start.31 = (f32[8,8]{1,0:T(8,128)S(1)}, f32[8,8]{1,0:T(8,128)S(1)}, u32[]{:S(2)}, u32[]{:S(2)}) collective-permute-start(f32[8,8]{1,0:T(8,128)S(1)} %add.134), channel_id=1, source_target_pairs={{0,16},{4,20},{8,24},{12,28},{16,0},{20,4},{24,8},{28,12},{1,17},{... | collective-permute-start | bytes 776 | tf_op jit(solution)/shard_map/ppermute | solution.py:266
  (187 shorter events, 53.1 us)
Async XLA Ops:
  6.5 103.0 %all-gather.3.cloned.1.call-start = ((), (), s32[]{:S(2)}) async-start(), calls=%async_computation.1 | async-start | bytes 17301504 | tf_op jit(solution)/shard_map/all_gather | solution.py:178
  8.2 13.5 %collective-permute-start.10 = (bf16[16,4096]{1,0:T(8,128)(2,1)S(1)}, bf16[16,4096]{1,0:T(8,128)(2,1)S(1)}, u32[]{:S(2)}, u32[]{:S(2)}) collective-permute-start(bf16[16,4096]{1,0:T(8,128)(2,1)S(1)} %dynamic-slice_bitcast_fusion.6), channel_id=1, source_target_pairs={{0,32},{32,0},{1,33},{33,1},{2,34},{34,2},{3,35},{35,3},{4,36},{36... | collective-permute-start | bytes 393224 | tf_op jit(solution)/shard_map/ppermute | solution.py:20
  10.4 13.5 %collective-permute-start = (bf16[48,3584]{1,0:T(8,128)(2,1)}, bf16[48,3584]{1,0:T(8,128)(2,1)}, u32[]{:S(2)}, u32[]{:S(2)}) collective-permute-start(bf16[48,3584]{1,0:T(8,128)(2,1)} %pad_maximum_fusion.14), channel_id=1, source_target_pairs={{0,3},{1,0},{2,1},{3,2},{4,7},{5,4},{6,5},{7,6},{8,11},{9,8},{10,9... | collective-permute-start | bytes 1032200 | tf_op jit(solution)/shard_map/ppermute | solution.py:20
  13.4 17.5 %collective-permute-start.1 = (bf16[48,3584]{1,0:T(8,128)(2,1)}, bf16[48,3584]{1,0:T(8,128)(2,1)}, u32[]{:S(2)}, u32[]{:S(2)}) collective-permute-start(bf16[48,3584]{1,0:T(8,128)(2,1)} %pad_maximum_fusion.15), channel_id=1, source_target_pairs={{0,2},{1,3},{2,0},{3,1},{4,6},{5,7},{6,4},{7,5},{8,10},{9,11},{10,... | collective-permute-start | bytes 1032200 | tf_op jit(solution)/shard_map/ppermute | solution.py:20
  14.9 21.4 %collective-permute-start.2 = (bf16[48,3584]{1,0:T(8,128)(2,1)}, bf16[48,3584]{1,0:T(8,128)(2,1)}, u32[]{:S(2)}, u32[]{:S(2)}) collective-permute-start(bf16[48,3584]{1,0:T(8,128)(2,1)} %pad_maximum_fusion.16), channel_id=1, source_target_pairs={{0,1},{1,2},{2,3},{3,0},{4,5},{5,6},{6,7},{7,4},{8,9},{9,10},{10,1... | collective-permute-start | bytes 1032200 | tf_op jit(solution)/shard_map/ppermute | solution.py:20
  21.8 24.0 %collective-permute-start.11 = (bf16[32,4096]{1,0:T(8,128)(2,1)S(1)}, bf16[32,4096]{1,0:T(8,128)(2,1)S(1)}, u32[]{:S(2)}, u32[]{:S(2)}) collective-permute-start(bf16[32,4096]{1,0:T(8,128)(2,1)S(1)} %pad_maximum_fusion.17), channel_id=1, source_target_pairs={{0,1},{1,2},{2,3},{3,0},{4,5},{5,6},{6,7},{7,4},{8,9},{9,10},{10,1... | collective-permute-start | bytes 786440 | tf_op jit(solution)/shard_map/ppermute | solution.py:20
  23.5 18.5 %collective-permute-start.12 = (bf16[32,4096]{1,0:T(8,128)(2,1)S(1)}, bf16[32,4096]{1,0:T(8,128)(2,1)S(1)}, u32[]{:S(2)}, u32[]{:S(2)}) collective-permute-start(bf16[32,4096]{1,0:T(8,128)(2,1)S(1)} %pad_maximum_fusion.17), channel_id=1, source_target_pairs={{0,3},{1,0},{2,1},{3,2},{4,7},{5,4},{6,5},{7,6},{8,11},{9,8},{10,9... | collective-permute-start | bytes 786440 | tf_op jit(solution)/shard_map/ppermute | solution.py:20
  23.9 17.5 %collective-permute-start.13 = (bf16[32,4096]{1,0:T(8,128)(2,1)S(1)}, bf16[32,4096]{1,0:T(8,128)(2,1)S(1)}, u32[]{:S(2)}, u32[]{:S(2)}) collective-permute-start(bf16[32,4096]{1,0:T(8,128)(2,1)S(1)} %pad_maximum_fusion.17), channel_id=1, source_target_pairs={{0,64},{64,128},{128,192},{192,0},{1,65},{65,129},{129,193},{193,1... | collective-permute-start | bytes 786440 | tf_op jit(solution)/shard_map/ppermute | solution.py:20
  31.0 14.9 %collective-permute-start.14 = (bf16[32,4096]{1,0:T(8,128)(2,1)S(1)}, bf16[32,4096]{1,0:T(8,128)(2,1)S(1)}, u32[]{:S(2)}, u32[]{:S(2)}) collective-permute-start(bf16[32,4096]{1,0:T(8,128)(2,1)S(1)} %pad_maximum_fusion.17), channel_id=1, source_target_pairs={{0,192},{64,0},{128,64},{192,128},{1,193},{65,1},{129,65},{193,129... | collective-permute-start | bytes 786440 | tf_op jit(solution)/shard_map/ppermute | solution.py:20
  38.2 14.4 %collective-permute-start.4 = (f32[200,128]{1,0:T(8,128)S(1)}, f32[200,128]{1,0:T(8,128)S(1)}, u32[]{:S(2)}, u32[]{:S(2)}) collective-permute-start(f32[200,128]{1,0:T(8,128)S(1)} %constant_dynamic-update-slice_fusion), channel_id=1, source_target_pairs={{0,2},{1,3},{2,0},{3,1},{4,6},{5,7},{6,4},{7,5},{8,10},{9,11},{10,... | collective-permute-start | bytes 307208 | tf_op jit(solution)/shard_map/ppermute | solution.py:20
  45.9 14.1 %collective-permute-start.18 = (bf16[48,4096]{1,0:T(8,128)(2,1)S(1)}, bf16[48,4096]{1,0:T(8,128)(2,1)S(1)}, u32[]{:S(2)}, u32[]{:S(2)}) collective-permute-start(bf16[48,4096]{1,0:T(8,128)(2,1)S(1)} %get-tuple-element.37), channel_id=1, source_target_pairs={{0,64},{64,128},{128,192},{192,0},{1,65},{65,129},{129,193},{193,1... | collective-permute-start | bytes 1179656 | tf_op jit(solution)/shard_map/ppermute | solution.py:20
  47.6 9.4 %collective-permute-start.19 = (bf16[48,4096]{1,0:T(8,128)(2,1)S(1)}, bf16[48,4096]{1,0:T(8,128)(2,1)S(1)}, u32[]{:S(2)}, u32[]{:S(2)}) collective-permute-start(bf16[48,4096]{1,0:T(8,128)(2,1)S(1)} %get-tuple-element.38), channel_id=1, source_target_pairs={{0,192},{64,0},{128,64},{192,128},{1,193},{65,1},{129,65},{193,129... | collective-permute-start | bytes 1179656 | tf_op jit(solution)/shard_map/ppermute | solution.py:20
  49.4 14.8 %collective-permute-start.16 = (bf16[48,4096]{1,0:T(8,128)(2,1)S(1)}, bf16[48,4096]{1,0:T(8,128)(2,1)S(1)}, u32[]{:S(2)}, u32[]{:S(2)}) collective-permute-start(bf16[48,4096]{1,0:T(8,128)(2,1)S(1)} %get-tuple-element.34), channel_id=1, source_target_pairs={{0,1},{1,2},{2,3},{3,0},{4,5},{5,6},{6,7},{7,4},{8,9},{9,10},{10,1... | collective-permute-start | bytes 1179656 | tf_op jit(solution)/shard_map/ppermute | solution.py:20
  51.3 12.9 %collective-permute-start.17 = (bf16[48,4096]{1,0:T(8,128)(2,1)S(1)}, bf16[48,4096]{1,0:T(8,128)(2,1)S(1)}, u32[]{:S(2)}, u32[]{:S(2)}) collective-permute-start(bf16[48,4096]{1,0:T(8,128)(2,1)S(1)} %get-tuple-element.33), channel_id=1, source_target_pairs={{0,3},{1,0},{2,1},{3,2},{4,7},{5,4},{6,5},{7,6},{8,11},{9,8},{10,9... | collective-permute-start | bytes 1179656 | tf_op jit(solution)/shard_map/ppermute | solution.py:20
  54.1 16.3 %collective-permute-start.7 = (bf16[2,208,128]{2,1,0:T(8,128)(2,1)S(1)}, bf16[2,208,128]{2,1,0:T(8,128)(2,1)S(1)}, u32[]{:S(2)}, u32[]{:S(2)}) collective-permute-start(bf16[2,208,128]{2,1,0:T(8,128)(2,1)S(1)} %get-tuple-element.50), channel_id=1, source_target_pairs={{0,192},{64,0},{128,64},{192,128},{1,193},{65,1},{129,65},{193,129... | collective-permute-start | bytes 319496 | tf_op jit(solution)/shard_map/ppermute | solution.py:20
  56.9 16.1 %collective-permute-start.8 = (bf16[2,208,128]{2,1,0:T(8,128)(2,1)S(1)}, bf16[2,208,128]{2,1,0:T(8,128)(2,1)S(1)}, u32[]{:S(2)}, u32[]{:S(2)}) collective-permute-start(bf16[2,208,128]{2,1,0:T(8,128)(2,1)S(1)} %get-tuple-element.50), channel_id=1, source_target_pairs={{0,128},{64,192},{128,0},{192,64},{1,129},{65,193},{129,1},{193,65... | collective-permute-start | bytes 319496 | tf_op jit(solution)/shard_map/ppermute | solution.py:20
  60.0 15.1 %collective-permute-start.9 = (bf16[2,208,128]{2,1,0:T(8,128)(2,1)S(1)}, bf16[2,208,128]{2,1,0:T(8,128)(2,1)S(1)}, u32[]{:S(2)}, u32[]{:S(2)}) collective-permute-start(bf16[2,208,128]{2,1,0:T(8,128)(2,1)S(1)} %get-tuple-element.50), channel_id=1, source_target_pairs={{0,64},{64,128},{128,192},{192,0},{1,65},{65,129},{129,193},{193,1... | collective-permute-start | bytes 319496 | tf_op jit(solution)/shard_map/ppermute | solution.py:20
  65.2 24.7 %collective-permute-start.22 = (bf16[32,4096]{1,0:T(8,128)(2,1)}, bf16[32,4096]{1,0:T(8,128)(2,1)}, u32[]{:S(2)}, u32[]{:S(2)}) collective-permute-start(bf16[32,4096]{1,0:T(8,128)(2,1)} %get-tuple-element.46), channel_id=1, source_target_pairs={{0,64},{64,128},{128,192},{192,0},{1,65},{65,129},{129,193},{193,1... | collective-permute-start | bytes 786440 | tf_op jit(solution)/shard_map/ppermute | solution.py:20
  67.6 16.9 %collective-permute-start.20 = (bf16[32,4096]{1,0:T(8,128)(2,1)}, bf16[32,4096]{1,0:T(8,128)(2,1)}, u32[]{:S(2)}, u32[]{:S(2)}) collective-permute-start(bf16[32,4096]{1,0:T(8,128)(2,1)} %get-tuple-element.48), channel_id=1, source_target_pairs={{0,1},{1,2},{2,3},{3,0},{4,5},{5,6},{6,7},{7,4},{8,9},{9,10},{10,1... | collective-permute-start | bytes 786440 | tf_op jit(solution)/shard_map/ppermute | solution.py:20
  70.4 17.4 %collective-permute-start.21 = (bf16[32,4096]{1,0:T(8,128)(2,1)}, bf16[32,4096]{1,0:T(8,128)(2,1)}, u32[]{:S(2)}, u32[]{:S(2)}) collective-permute-start(bf16[32,4096]{1,0:T(8,128)(2,1)} %get-tuple-element.47), channel_id=1, source_target_pairs={{0,3},{1,0},{2,1},{3,2},{4,7},{5,4},{6,5},{7,6},{8,11},{9,8},{10,9... | collective-permute-start | bytes 786440 | tf_op jit(solution)/shard_map/ppermute | solution.py:20
  73.1 19.4 %collective-permute-start.23 = (bf16[32,4096]{1,0:T(8,128)(2,1)}, bf16[32,4096]{1,0:T(8,128)(2,1)}, u32[]{:S(2)}, u32[]{:S(2)}) collective-permute-start(bf16[32,4096]{1,0:T(8,128)(2,1)} %get-tuple-element.45), channel_id=1, source_target_pairs={{0,192},{64,0},{128,64},{192,128},{1,193},{65,1},{129,65},{193,129... | collective-permute-start | bytes 786440 | tf_op jit(solution)/shard_map/ppermute | solution.py:20
  76.2 22.8 %collective-permute-start.15 = (bf16[4096,256]{1,0:T(8,128)(2,1)}, bf16[4096,256]{1,0:T(8,128)(2,1)}, u32[]{:S(2)}, u32[]{:S(2)}) collective-permute-start(bf16[4096,256]{1,0:T(8,128)(2,1)} %get-tuple-element.12), channel_id=1, source_target_pairs={{0,32},{32,0},{1,33},{33,1},{2,34},{34,2},{3,35},{35,3},{4,36},{36... | collective-permute-start | bytes 6291464 | tf_op jit(solution)/shard_map/ppermute | solution.py:20
  85.3 13.4 %collective-permute-start.24 = (bf16[8,4096]{1,0:T(8,128)(2,1)S(1)}, bf16[8,4096]{1,0:T(8,128)(2,1)S(1)}, u32[]{:S(2)}, u32[]{:S(2)}) collective-permute-start(bf16[8,4096]{1,0:T(8,128)(2,1)S(1)} %slice.233), channel_id=1, source_target_pairs={{0,1},{1,2},{2,3},{3,0},{4,5},{5,6},{6,7},{7,4},{8,9},{9,10},{10,1... | collective-permute-start | bytes 196616 | tf_op jit(solution)/shard_map/ppermute | solution.py:20
  88.7 10.1 %collective-permute-start.25 = (bf16[8,4096]{1,0:T(8,128)(2,1)S(1)}, bf16[8,4096]{1,0:T(8,128)(2,1)S(1)}, u32[]{:S(2)}, u32[]{:S(2)}) collective-permute-start(bf16[8,4096]{1,0:T(8,128)(2,1)S(1)} %slice.234), channel_id=1, source_target_pairs={{0,3},{1,0},{2,1},{3,2},{4,7},{5,4},{6,5},{7,6},{8,11},{9,8},{10,9... | collective-permute-start | bytes 196616 | tf_op jit(solution)/shard_map/ppermute | solution.py:20
  (36 other events, 291.1 us)
Sparse Core Ops, SparseCore 0:
  9.9 98.8 all-gather.2
